TPU v7x, 32 devices: a whole 2x2x4 slice. The times are simulated.
32 devices in a mesh: real: 4 (over y, x), cell: 8 (over z, core).
Axes of the slice: x: 2, y: 2, z: 4, core: 2. Of those that a mesh axis runs over, the one named last changes fastest.
Arguments:
- soil_heat_field: float32 [256, 256, 512], P('cell', None, 'real'), may hold values from -250 to 250, as said below
- seed_subspace: float32 [512, 128], replicated, may hold values from -6 to 6
Outputs:
- core_tensor: float32 [256, 256, 128], P('cell', None, 'real')
- mode_factor: float32 [512, 128], replicated
- triangle: float32 [512, 512], replicated
Inputs may be any that keep to these rules, and one draw needn't show every extreme that they name: `soil_heat_field`: real values.
All inputs are finite; a program needn't handle non-finite values.
Results may differ from a plain program's by a relative error of at most 0.00024.
Values sent between devices are 32-bit elements; how exact they have to be, the bound alone decides.
A program may use at most 64 MiB of HBM per device.

v0:
```python
import jax
import jax.numpy as jnp
from jax import lax
from jax.sharding import PartitionSpec as P

ITERS = 3


def swapped(block, axis, stride):
    count = lax.axis_size(axis)
    route = []
    for low in range(count):
        high = low | 1 << stride
        if high != low and high < count:
            route += [(low, high), (high, low)]
    return lax.ppermute(block, axis, route)


def gram_of(array_operand):
    return lax.dot_general(
        array_operand,
        array_operand,
        (((0,), (0,)), ((), ())),
        precision=lax.Precision.HIGHEST,
        preferred_element_type=jnp.float32,
    )


def orthonormal(gram, seed_subspace):
    basis_block = seed_subspace
    for step_index in range(ITERS):
        imaged = jnp.dot(
            gram, basis_block, precision=lax.Precision.HIGHEST, preferred_element_type=jnp.float32
        )
        cholesky_lower = jnp.linalg.cholesky(gram_of(imaged))
        basis_block = lax.linalg.triangular_solve(
            cholesky_lower, imaged, left_side=False, lower=True, transpose_a=True
        )
    return basis_block


def local(soil_heat_field, seed_subspace):
    permuted_array = lax.all_to_all(
        soil_heat_field, "real", split_axis=1, concat_axis=2, tiled=True
    )
    flattened_mode_array = permuted_array.reshape(-1, permuted_array.shape[2])
    total_rows = flattened_mode_array.shape[0] * lax.axis_size(("real", "cell"))
    own_gram = gram_of(flattened_mode_array) / total_rows
    summed = own_gram
    for level in range(lax.axis_size(("real", "cell")).bit_length() - 1):
        summed = summed + swapped(summed, ("real", "cell"), level)
    triangle = jnp.linalg.cholesky(summed).T
    mode_factor = orthonormal(summed, seed_subspace)
    compressed_array = jnp.dot(
        flattened_mode_array,
        mode_factor,
        precision=lax.Precision.HIGHEST,
        preferred_element_type=jnp.float32,
    )
    compressed_array = compressed_array.reshape(
        permuted_array.shape[0], permuted_array.shape[1], -1
    )
    core_tensor = lax.all_to_all(compressed_array, "real", split_axis=2, concat_axis=1, tiled=True)
    return (core_tensor, mode_factor, triangle)


def solution(mesh):
    return jax.shard_map(
        local,
        mesh=mesh,
        in_specs=(P("cell", None, "real"), P()),
        out_specs=(P("cell", None, "real"), P(), P()),
        check_vma=False,
    )
```

profile of v0, /device:TPU:0, one launch (start us, length us, event | category | flops | bytes accessed | tf_op | source)
XLA Modules:
  0.0 394.4 jit_solution(227310483635947209)
XLA Ops:
  0.6 4.7 %copy.44 = f32[32,256,128]{2,0,1:T(8,128)S(1)} copy(f32[32,256,128]{2,1,0:T(8,128)} %param.5) | data formatting | bytes 8388608 | tf_op args[0]
  5.3 52.8 %all_to_all.33 = f32[32,256,128]{2,0,1:T(8,128)S(1)} all-to-all(f32[32,256,128]{2,0,1:T(8,128)S(1)} %copy.44), channel_id=1, replica_groups=mesh['real'=4,'cell'=8] {'real'}, dimensions={1} | all-to-all | bytes 8388608 | tf_op jit(solution)/shard_map/all_to_all | solution.py:43
  60.8 6.8 %fusion.9 = f32[512,512]{0,1:T(8,128)S(1)} fusion(f32[256,8,4,128]{3,2,1,0:T(4,128)S(1)} %bitcast.96), kind=kOutput, calls=%fused_computation.7 | convolution fusion | flops 6442713088 | bytes 5242880 | tf_op jit(solution)/shard_map/dot_general | solution.py:20
  72.2 23.6 %collective-permute-done.1 = f32[512,512]{0,1:T(8,128)S(1)} collective-permute-done((f32[512,512]{0,1:T(8,128)S(1)}, f32[512,512]{0,1:T(8,128)S(1)}, u32[]{:S(2)}, u32[]{:S(2)}) %collective-permute-start.1) | collective-permute-done | bytes 1048608 | tf_op jit(solution)/shard_map/ppermute | solution.py:16
  98.7 45.2 %collective-permute-done.2 = f32[512,512]{0,1:T(8,128)S(1)} collective-permute-done((f32[512,512]{0,1:T(8,128)S(1)}, f32[512,512]{0,1:T(8,128)S(1)}, u32[]{:S(2)}, u32[]{:S(2)}) %collective-permute-start.2) | collective-permute-done | bytes 1048608 | tf_op jit(solution)/shard_map/ppermute | solution.py:16
  145.1 23.1 %collective-permute-done.3 = f32[512,512]{0,1:T(8,128)S(1)} collective-permute-done((f32[512,512]{0,1:T(8,128)S(1)}, f32[512,512]{0,1:T(8,128)S(1)}, u32[]{:S(2)}, u32[]{:S(2)}) %collective-permute-start.3) | collective-permute-done | bytes 1048608 | tf_op jit(solution)/shard_map/ppermute | solution.py:16
  169.4 22.2 %collective-permute-done.4 = f32[512,512]{0,1:T(8,128)S(1)} collective-permute-done((f32[512,512]{0,1:T(8,128)S(1)}, f32[512,512]{0,1:T(8,128)S(1)}, u32[]{:S(2)}, u32[]{:S(2)}) %collective-permute-start.4) | collective-permute-done | bytes 1048608 | tf_op jit(solution)/shard_map/ppermute | solution.py:16
  194.5 11.7 %cholesky.325 = f32[128,128]{1,0:T(8,128)S(1)} custom-call(f32[128,128]{1,0:T(8,128)S(1)} %fusion.37), custom_call_target="Cholesky" | custom-call | tf_op jit(solution)/shard_map/jit(cholesky)/cholesky | solution.py:35
  207.5 9.8 %custom-call.37 = f32[1,128,128]{1,2,0:T(8,128)S(1)} custom-call(f32[1,128,128]{2,1,0:T(8,128)S(1)} %fusion.21), custom_call_target="InvertDiagBlocksLowerTriangular" | custom-call | tf_op jit(solution)/shard_map/triangular_solve/custom-call.8 | solution.py:36
  220.3 12.1 %cholesky.336 = f32[128,128]{1,0:T(8,128)S(1)} custom-call(f32[128,128]{1,0:T(8,128)S(1)} %fusion.35), custom_call_target="Cholesky" | custom-call | tf_op jit(solution)/shard_map/jit(cholesky)/cholesky | solution.py:35
  233.7 9.8 %custom-call.38 = f32[1,128,128]{1,2,0:T(8,128)S(1)} custom-call(f32[1,128,128]{2,1,0:T(8,128)S(1)} %fusion.22), custom_call_target="InvertDiagBlocksLowerTriangular" | custom-call | tf_op jit(solution)/shard_map/triangular_solve/custom-call.8 | solution.py:36
  246.5 11.7 %cholesky.347 = f32[128,128]{1,0:T(8,128)S(1)} custom-call(f32[128,128]{1,0:T(8,128)S(1)} %fusion.33), custom_call_target="Cholesky" | custom-call | tf_op jit(solution)/shard_map/jit(cholesky)/cholesky | solution.py:35
  259.5 9.9 %custom-call.39 = f32[1,128,128]{1,2,0:T(8,128)S(1)} custom-call(f32[1,128,128]{2,1,0:T(8,128)S(1)} %fusion.23), custom_call_target="InvertDiagBlocksLowerTriangular" | custom-call | tf_op jit(solution)/shard_map/triangular_solve/custom-call.8 | solution.py:36
  269.9 6.6 %fusion.6 = f32[2048,128]{0,1:T(8,128)S(1)} fusion(f32[512,128]{0,1:T(8,128)S(1)} %convolution_bitcast_fusion, f32[256,8,4,128]{3,2,1,0:T(4,128)} %bitcast.97), kind=kOutput, calls=%fused_computation.6 | convolution fusion | flops 1610612736 | bytes 5505024 | tf_op jit(solution)/shard_map/dot_general | solution.py:54
  285.4 3.7 all-to-all-start.1
  290.6 11.7 %cholesky.131 = f32[128,128]{1,0:T(8,128)S(1)} custom-call(f32[128,128]{1,0:T(8,128)S(1)} %cholesky.356), custom_call_target="Cholesky" | custom-call | tf_op jit(solution)/shard_map/jit(cholesky)/cholesky | solution.py:52
  302.5 9.8 %custom-call.32 = f32[1,128,128]{1,2,0:T(8,128)S(1)} custom-call(f32[1,128,128]{2,1,0:T(8,128)S(1)} %get-tuple-element.29), custom_call_target="InvertDiagBlocksLowerTriangular" | custom-call | tf_op jit(solution)/shard_map/jit(cholesky)/cholesky | solution.py:52
  313.7 11.7 %cholesky.244 = f32[128,128]{1,0:T(8,128)S(1)} custom-call(f32[128,128]{1,0:T(8,128)S(1)} %cholesky.360), custom_call_target="Cholesky" | custom-call | tf_op jit(solution)/shard_map/jit(cholesky)/cholesky | solution.py:52
  325.4 10.2 %custom-call.33 = f32[1,128,128]{1,2,0:T(8,128)S(1)} custom-call(f32[1,128,128]{2,1,0:T(8,128)S(1)} %get-tuple-element.26), custom_call_target="InvertDiagBlocksLowerTriangular" | custom-call | tf_op jit(solution)/shard_map/jit(cholesky)/cholesky | solution.py:52
  337.8 13.2 %cholesky.265 = f32[128,128]{1,0:T(8,128)} custom-call(f32[128,128]{1,0:T(8,128)} %cholesky.365), custom_call_target="Cholesky" | custom-call | tf_op jit(solution)/shard_map/jit(cholesky)/cholesky | solution.py:52
  352.4 11.3 %custom-call.34 = f32[1,128,128]{1,2,0:T(8,128)} custom-call(f32[1,128,128]{2,1,0:T(8,128)} %get-tuple-element.23), custom_call_target="InvertDiagBlocksLowerTriangular" | custom-call | tf_op jit(solution)/shard_map/jit(cholesky)/cholesky | solution.py:52
  365.1 11.7 %cholesky.282 = f32[128,128]{1,0:T(8,128)S(1)} custom-call(f32[128,128]{1,0:T(8,128)S(1)} %slice_subtract_fusion.2), custom_call_target="Cholesky" | custom-call | tf_op jit(solution)/shard_map/jit(cholesky)/cholesky | solution.py:52
  383.7 3.7 reduce.28
  391.1 3.2 all_to_all.30
  (71 shorter events, 50.5 us)
Async XLA Ops:
  0.6 191.1 %copy-start = (f32[512,128]{1,0:T(8,128)S(1)}, f32[512,128]{1,0:T(8,128)}, u32[]{:S(2)}) copy-start(f32[512,128]{1,0:T(8,128)} %param.6) | copy-start | bytes 786436
  60.8 9.8 %copy-start.1 = (f32[32,4,64,128]{3,1,2,0:T(4,128)}, f32[32,4,64,128]{3,1,2,0:T(4,128)S(1)}, u32[]{:S(2)}) copy-start(f32[32,4,64,128]{3,1,2,0:T(4,128)S(1)} %copy.45) | copy-start | bytes 12582916
  67.7 2.7 collective-permute-start
  70.6 25.3 %collective-permute-start.1 = (f32[512,512]{0,1:T(8,128)S(1)}, f32[512,512]{0,1:T(8,128)S(1)}, u32[]{:S(2)}, u32[]{:S(2)}) collective-permute-start(f32[512,512]{0,1:T(8,128)S(1)} %add.61), channel_id=1, source_target_pairs={{0,2},{2,0},{1,3},{3,1},{4,6},{6,4},{5,7},{7,5},{8,10},{10,8},{9,1... | collective-permute-start | bytes 3145736 | tf_op jit(solution)/shard_map/ppermute | solution.py:16
  96.1 47.8 %collective-permute-start.2 = (f32[512,512]{0,1:T(8,128)S(1)}, f32[512,512]{0,1:T(8,128)S(1)}, u32[]{:S(2)}, u32[]{:S(2)}) collective-permute-start(f32[512,512]{0,1:T(8,128)S(1)} %add.62), channel_id=1, source_target_pairs={{0,4},{4,0},{1,5},{5,1},{2,6},{6,2},{3,7},{7,3},{8,12},{12,8},{9,1... | collective-permute-start | bytes 3145736 | tf_op jit(solution)/shard_map/ppermute | solution.py:16
  144.1 24.1 %collective-permute-start.3 = (f32[512,512]{0,1:T(8,128)S(1)}, f32[512,512]{0,1:T(8,128)S(1)}, u32[]{:S(2)}, u32[]{:S(2)}) collective-permute-start(f32[512,512]{0,1:T(8,128)S(1)} %add.63), channel_id=1, source_target_pairs={{0,8},{8,0},{1,9},{9,1},{2,10},{10,2},{3,11},{11,3},{4,12},{12,4},... | collective-permute-start | bytes 3145736 | tf_op jit(solution)/shard_map/ppermute | solution.py:16
  168.4 23.1 %collective-permute-start.4 = (f32[512,512]{0,1:T(8,128)S(1)}, f32[512,512]{0,1:T(8,128)S(1)}, u32[]{:S(2)}, u32[]{:S(2)}) collective-permute-start(f32[512,512]{0,1:T(8,128)S(1)} %add.64), channel_id=1, source_target_pairs={{0,16},{16,0},{1,17},{17,1},{2,18},{18,2},{3,19},{19,3},{4,20},{20... | collective-permute-start | bytes 3145736 | tf_op jit(solution)/shard_map/ppermute | solution.py:16
  285.4 97.7 %all-to-all-start.1 = ((f32[4,1,65536]{2,1,0:T(1,128)}), f32[4,1,65536]{2,1,0:T(1,128)S(1)}, u32[]{:S(2)}, u32[]{:S(2)}) async-start(f32[4,1,65536]{2,1,0:T(1,128)} %reshape.63), calls=%async_computation.1 | async-start | bytes 2097152 | tf_op jit(solution)/shard_map/all_to_all | solution.py:63
  313.0 0.7 copy-start.2
where the time goes:
time: 399 us; the launch traced here: 394 us
  other arithmetic  159 us (40%)
  waiting for transfers between devices  117 us (29%)
  blocking collectives  52.8 us (13%)
  local copies, waits for them, and re-layouts  26.7 us (7%)
  matrix products  25.6 us (6%)
  starting transfers between devices  10.1 us (3%)
    ppermute x5, waiting for transfers between devices, swapped(): return lax.ppermute(block, axis, route)  117 us
    another operation x14, other arithmetic, local(): triangle = jnp.linalg.cholesky(summed).T  83.2 us
    all_to_all x1, blocking collectives, local(): lax.all_to_all(soil_heat_field, 'real', split_axis=1, concat_axis=2, tile...  52.8 us
    another operation x9, other arithmetic, orthonormal(): cholesky_lower = jnp.linalg.cholesky(gram_of(imaged))  37.6 us
    another operation x6, other arithmetic, orthonormal(): lax.linalg.triangular_solve(cholesky_lower, imaged, left_side=False, lowe...  31.5 us
    unnamed x11, local copies, waits for them, and re-layouts  10.9 us
    dot_general x4, matrix products, gram_of(): lax.dot_general(array_operand, array_operand, (((0,), (0,)), ((), ())), p...  8.59 us
  transfers between devices with their start and end apart: 6, of which 6 were waited for; matrix products, arithmetic and copies ran while one was open for 23% of the time, Pallas kernels for 0%

commit v1 on v0

v1 whole, which is shorter than its diff:
```python
import functools
import jax
import jax.numpy as jnp
from jax import lax
from jax.experimental import pallas as pl
from jax.experimental.pallas import tpu as pltpu
from jax.sharding import PartitionSpec as P

ITERS = 3
PANEL = 32
GROUP = 8
HI = lax.Precision.HIGHEST


def mm(a, b, dims=((1,), (0,))):
    return lax.dot_general(
        a, b, (dims, ((), ())), precision=HI, preferred_element_type=jnp.float32
    )


def eliminate(panel, first_lane):
    size = panel.shape[0]
    done, pivots = [], []
    rest = panel
    for g in range(0, size, GROUP):
        rows = [rest[i : i + 1, :] for i in range(GROUP)]
        lane = first_lane + g
        cell = {
            (i, k): rows[i][:, lane + k : lane + k + 1]
            for i in range(GROUP)
            for k in range(i, GROUP)
        }
        below = rest[GROUP:, :]
        more = below.shape[0] > 0
        if more:
            cols = [below[:, lane + k : lane + k + 1] for k in range(GROUP)]
        for i in range(GROUP):
            inverse = 1.0 / cell[i, i]
            pivots.append(cell[i, i])
            for k in range(i + 1, GROUP):
                factor = cell[i, k] * inverse
                for q in range(k, GROUP):
                    cell[k, q] = cell[k, q] - factor * cell[i, q]
                rows[k] = rows[k] - factor * rows[i]
                if more:
                    cols[k] = cols[k] - cols[i] * factor
            if more:
                below = below - cols[i] * (rows[i] * inverse)
        done += rows
        rest = below
    return [u * lax.rsqrt(p) for u, p in zip(done, pivots)]


def factor_panels(works, outs, size):
    for p in range(0, size, PANEL):
        for work, out in zip(works, outs):
            rows = jnp.concatenate(eliminate(work[p : p + PANEL, :], p), axis=0)
            out[p : p + PANEL, :] = rows
            if p + PANEL < size:
                left = size - p - PANEL
                drop = mm(rows[:, :size], rows, ((0,), (0,)))
                work[p + PANEL :, :] = work[p + PANEL :, :] - drop[p + PANEL :, :]


def factors_kernel(gram_ref, seed_ref, basis_ref, tri_ref, rest, image, work_a, out_a, work_b, out_b):
    size = seed_ref.shape[1]
    total = gram_ref.shape[0]
    row = lax.broadcasted_iota(jnp.int32, (size, size), 0)
    col = lax.broadcasted_iota(jnp.int32, (size, size), 1)
    eye = jnp.where(row == col, 1.0, 0.0).astype(jnp.float32)
    rest[...] = gram_ref[...]
    basis_ref[...] = seed_ref[...]

    def triangle_start(block):
        at = pl.multiple_of(block * size, size)
        work_b[:, :size] = rest[pl.ds(at, size), pl.ds(at, size)]
        work_b[:, size:] = eye

    def triangle_end(block):
        at = pl.multiple_of(block * size, size)
        inverse = jnp.where(row >= col, out_b[:, size:], 0.0)
        strip = mm(inverse, rest[pl.ds(at, size), :])
        rows = at + lax.broadcasted_iota(jnp.int32, (size, total), 0)
        cols = lax.broadcasted_iota(jnp.int32, (size, total), 1)
        strip = jnp.where(cols >= rows, strip, 0.0)
        tri_ref[pl.ds(at, size), :] = strip
        return strip

    def step(index, carry):
        image[...] = mm(gram_ref[...], basis_ref[...])
        work_a[:, :size] = mm(image[...], image[...], ((0,), (0,)))
        work_a[:, size:] = eye
        triangle_start(index)
        factor_panels([work_a, work_b], [out_a, out_b], size)
        inverse = jnp.where(row >= col, out_a[:, size:], 0.0)
        basis_ref[...] = mm(image[...], inverse, ((1,), (1,)))
        strip = triangle_end(index)
        rest[...] = rest[...] - mm(strip, strip, ((0,), (0,)))
        return carry

    blocks = total // size
    lax.fori_loop(0, ITERS, step, 0)
    for block in range(ITERS, blocks):
        triangle_start(block)
        factor_panels([work_b], [out_b], size)
        strip = triangle_end(block)
        if block + 1 < blocks:
            rest[...] = rest[...] - mm(strip, strip, ((0,), (0,)))


def factors(gram, seed_subspace):
    total, size = seed_subspace.shape
    vmem = pl.BlockSpec(memory_space=pltpu.VMEM)
    return pl.pallas_call(
        factors_kernel,
        out_shape=(
            jax.ShapeDtypeStruct((total, size), jnp.float32),
            jax.ShapeDtypeStruct((total, total), jnp.float32),
        ),
        in_specs=[vmem] * 2,
        out_specs=[vmem] * 2,
        scratch_shapes=[
            pltpu.VMEM((total, total), jnp.float32),
            pltpu.VMEM((total, size), jnp.float32),
        ]
        + [pltpu.VMEM((size, 2 * size), jnp.float32)] * 4,
        compiler_params=pltpu.CompilerParams(vmem_limit_bytes=32 * 1024 * 1024),
    )(gram, seed_subspace)


def local(soil_heat_field, seed_subspace):
    permuted_array = lax.all_to_all(
        soil_heat_field, "real", split_axis=1, concat_axis=2, tiled=True
    )
    flat = permuted_array.reshape(-1, permuted_array.shape[2])
    total_rows = flat.shape[0] * lax.axis_size(("real", "cell"))
    summed = lax.psum(mm(flat, flat, ((0,), (0,))) / total_rows, ("real", "cell"))
    mode_factor, triangle = factors(summed, seed_subspace)
    compressed = mm(flat, mode_factor).reshape(
        permuted_array.shape[0], permuted_array.shape[1], -1
    )
    core_tensor = lax.all_to_all(compressed, "real", split_axis=2, concat_axis=1, tiled=True)
    return (core_tensor, mode_factor, triangle)


def solution(mesh):
    return jax.shard_map(
        local,
        mesh=mesh,
        in_specs=(P("cell", None, "real"), P()),
        out_specs=(P("cell", None, "real"), P(), P()),
        check_vma=False,
    )
```

time: 399 us -> 354 us (0.89)
  other arithmetic: 159 us -> 3.68 us
  Pallas kernels: 0 us -> 97.8 us
  blocking collectives: 52.8 us -> 69 us
  waiting for transfers between devices: 117 us -> 130 us
  matrix products: 25.6 us -> 14.6 us
  between operations: 3.83 us -> 14.3 us
  starting transfers between devices: 10.1 us -> 0.04 us
  local copies, waits for them, and re-layouts: 26.7 us -> 21.6 us
    another operation x29 -> x0, other arithmetic: 152 us -> none  [the longest x14 83.2 us: local(): triangle = jnp.linalg.cholesky(summed).T]
    psum x0 -> x1, waiting for transfers between devices: none -> 130 us  [local(): lax.psum(mm(flat, flat, ((0,), (0,))) / total_rows, ('real', 'cell'))]
    ppermute x5 -> x0, waiting for transfers between devices: 117 us -> none  [swapped(): return lax.ppermute(block, axis, route)]
    pallas_call x0 -> x1, Pallas kernels: none -> 97.8 us  [factors(): pl.pallas_call(factors_kernel, out_shape=(jax.ShapeDtypeStruct((total, si...]
    all_to_all x0 -> x1, blocking collectives: none -> 16 us  [local(): lax.all_to_all(compressed, 'real', split_axis=2, concat_axis=1, tiled=True)]
    ppermute x5 -> x0, starting transfers between devices: 6.32 us -> none  [swapped(): return lax.ppermute(block, axis, route)]
    dot_general x8 -> x2, matrix products: 20.8 us -> 14.6 us  [mm(): lax.dot_general(a, b, (dims, ((), ())), precision=HI, preferred_element_t...]
    another operation x9 -> x0, matrix products: 4.85 us -> none  [the longest x6 3.6 us: local(): triangle = jnp.linalg.cholesky(summed).T]
  transfers between devices with their start and end apart: 6 -> 1, of which waited for: 6 -> 1; matrix products, arithmetic and copies ran while one was open for 23% -> 0% of each run, Pallas kernels for 0% -> 0%
where the time goes in v1:
time: 354 us; the launch traced here: 351 us
  waiting for transfers between devices  130 us (37%)
  Pallas kernels  97.8 us (28%)
  blocking collectives  69 us (19%)
  local copies, waits for them, and re-layouts  21.6 us (6%)
  matrix products  14.6 us (4%)
  between operations  14.3 us (4%)
  other arithmetic  3.68 us (1%)
    psum x1, waiting for transfers between devices, local(): lax.psum(mm(flat, flat, ((0,), (0,))) / total_rows, ('real', 'cell'))  130 us
    pallas_call x1, Pallas kernels, factors(): pl.pallas_call(factors_kernel, out_shape=(jax.ShapeDtypeStruct((total, si...  97.8 us
    all_to_all x1, blocking collectives, local(): lax.all_to_all(soil_heat_field, 'real', split_axis=1, concat_axis=2, tile...  53 us
    all_to_all x1, blocking collectives, local(): lax.all_to_all(compressed, 'real', split_axis=2, concat_axis=1, tiled=True)  16 us
    dot_general x2, matrix products, mm(): lax.dot_general(a, b, (dims, ((), ())), precision=HI, preferred_element_t...  14.6 us
    unnamed x9, local copies, waits for them, and re-layouts  10.1 us
  transfers between devices with their start and end apart: 1, of which 1 were waited for; matrix products, arithmetic and copies ran while one was open for 0% of the time, Pallas kernels for 0%

profile of v1, /device:TPU:0, one launch (start us, length us, event | category | flops | bytes accessed | tf_op | source)
XLA Modules:
  0.0 350.7 jit_solution(9201265753411016969)
XLA Ops:
  7.2 0.0 all-reduce.2.cloned.1.call-start
  7.2 4.6 %copy.16 = f32[32,256,128]{2,0,1:T(8,128)S(1)} copy(f32[32,256,128]{2,1,0:T(8,128)} %param.2) | data formatting | bytes 8388608 | tf_op args[0]
  11.8 53.0 %all_to_all.33 = f32[32,256,128]{2,0,1:T(8,128)S(1)} all-to-all(f32[32,256,128]{2,0,1:T(8,128)S(1)} %copy.16), channel_id=1, replica_groups=mesh['real'=4,'cell'=8] {'real'}, dimensions={1} | all-to-all | bytes 8388608 | tf_op jit(solution)/shard_map/all_to_all | solution.py:132
  64.8 2.7 copy.17
  67.5 0.0 copy-start.2
  67.6 1.9 copy-done.2
  69.5 0.0 copy-start.1
  69.5 7.8 %fusion.9 = f32[512,512]{1,0:T(8,128)} fusion(f32[256,8,4,128]{3,2,1,0:T(4,128)S(1)} %bitcast.24), kind=kOutput, calls=%fused_computation.7 | convolution fusion | flops 6442713088 | bytes 5242880 | tf_op jit(solution)/shard_map/dot_general | solution.py:16
  77.3 0.0 all-reduce.2.cloned.1.call-update
  77.3 129.7 %all-reduce.2.cloned.1.call-done.gram_ref = f32[512,512]{1,0:T(8,128)} async-done(((f32[512,512]{1,0:T(8,128)}), f32[512,512]{1,0:T(8,128)}) %all-reduce.2.cloned.1.call-update) | async-done | bytes 1048592 | tf_op jit(solution)/shard_map/psum | solution.py:137
  207.0 0.0 copy-done.1
  207.0 0.0 copy-start
  207.0 1.2 copy-done
  208.3 97.8 %shard_map.49 = (f32[512,128]{1,0:T(8,128)}, f32[512,512]{1,0:T(8,128)}) custom-call(f32[512,512]{1,0:T(8,128)S(1)} %copy-done, f32[512,128]{1,0:T(8,128)S(1)} %copy-done.1), custom_call_target="tpu_custom_call" | custom-call | tf_op jit(solution)/shard_map/pallas_call | solution.py:114
  306.1 6.8 %fusion.6 = f32[2048,128]{0,1:T(8,128)S(1)} fusion(f32[512,128]{1,0:T(8,128)} %get-tuple-element.3, f32[256,8,4,128]{3,2,1,0:T(4,128)} %bitcast.25), kind=kOutput, calls=%fused_computation.6 | convolution fusion | flops 1610612736 | bytes 5505024 | tf_op jit(solution)/shard_map/dot_general | solution.py:16
  312.8 0.3 copy.18
  313.2 2.0 copy.19
  315.2 1.4 reshape.15
  316.6 16.0 %all_to_all.34 = f32[4,1,65536]{2,1,0:T(1,128)S(1)} all-to-all(f32[4,1,65536]{2,1,0:T(1,128)S(1)} %reshape.15), channel_id=1, replica_groups=mesh['real'=4,'cell'=8] {'real'}, dimensions={0} | all-to-all | bytes 2097152 | tf_op jit(solution)/shard_map/all_to_all | solution.py:142
  332.5 0.5 broadcast.1
  333.1 3.7 %reduce = f32[4,65536]{1,0:T(4,128)S(1)} reduce(f32[4,1,65536]{2,1,0:T(1,128)S(1)} %all_to_all.34, f32[]{:T(128)} %broadcast.1), dimensions={1}, to_apply=%all_to_all.27.reduce_sub_computation | reduce | bytes 2097156 | tf_op jit(solution)/shard_map/all_to_all | solution.py:142
  336.7 1.0 reshape.16
  337.7 2.7 copy.21
  340.4 3.2 all_to_all.30
Async XLA Ops:
  7.2 199.9 %all-reduce.2.cloned.1.call-start = ((), (), s32[]{:S(2)}) async-start(), calls=%async_computation.2 | async-start | bytes 2097152 | tf_op jit(solution)/shard_map/psum | solution.py:137
  67.5 1.9 copy-start.2
  69.5 137.6 %copy-start.1 = (f32[512,128]{1,0:T(8,128)S(1)}, f32[512,128]{1,0:T(8,128)}, u32[]{:S(2)}) copy-start(f32[512,128]{1,0:T(8,128)} %seed_ref.1) | copy-start | bytes 786436
  207.0 1.2 copy-start
Sparse Core Ops, SparseCore 0:
  77.4 129.5 all-reduce.1

commit v2 on v1

--- a/solution.py
+++ b/solution.py
@@ -18,53 +18,78 @@
     )
 
 
-def eliminate(panel, first_lane):
-    size = panel.shape[0]
-    done, pivots = [], []
-    rest = panel
-    for g in range(0, size, GROUP):
-        rows = [rest[i : i + 1, :] for i in range(GROUP)]
-        lane = first_lane + g
+def upper_blocks(count):
+    return [(i, j) for i in range(count) for j in range(i, count)]
+
+
+def spread(tile, lane):
+    return jnp.broadcast_to(tile[:, lane : lane + 1], tile.shape)
+
+
+def eliminate(tiles, first_lane):
+    sub = lax.broadcasted_iota(jnp.int32, tiles[0][0].shape, 0)
+    done = []
+    for g in range(len(tiles)):
+        lane = first_lane + g * GROUP
+        head, rest = tiles[g], tiles[g + 1 :]
+        rows = [
+            [jnp.broadcast_to(half[i : i + 1, :], half.shape) for half in head]
+            for i in range(GROUP)
+        ]
         cell = {
-            (i, k): rows[i][:, lane + k : lane + k + 1]
+            (i, k): spread(rows[i][0], lane + k)
             for i in range(GROUP)
             for k in range(i, GROUP)
         }
-        below = rest[GROUP:, :]
-        more = below.shape[0] > 0
-        if more:
-            cols = [below[:, lane + k : lane + k + 1] for k in range(GROUP)]
+        cols = [[spread(t[0], lane + k) for t in rest] for k in range(GROUP)]
         for i in range(GROUP):
             inverse = 1.0 / cell[i, i]
-            pivots.append(cell[i, i])
             for k in range(i + 1, GROUP):
                 factor = cell[i, k] * inverse
                 for q in range(k, GROUP):
                     cell[k, q] = cell[k, q] - factor * cell[i, q]
-                rows[k] = rows[k] - factor * rows[i]
-                if more:
-                    cols[k] = cols[k] - cols[i] * factor
-            if more:
-                below = below - cols[i] * (rows[i] * inverse)
-        done += rows
-        rest = below
-    return [u * lax.rsqrt(p) for u, p in zip(done, pivots)]
+                rows[k] = [x - factor * y for x, y in zip(rows[k], rows[i])]
+                cols[k] = [x - factor * y for x, y in zip(cols[k], cols[i])]
+            scaled = [y * inverse for y in rows[i]]
+            rest = [
+                tuple(x - c * y for x, y in zip(t, scaled)) for t, c in zip(rest, cols[i])
+            ]
+        tiles = tiles[: g + 1] + rest
+        halves = []
+        for h in range(2):
+            value = rows[0][h] * lax.rsqrt(cell[0, 0])
+            for i in range(1, GROUP):
+                value = jnp.where(sub == i, rows[i][h] * lax.rsqrt(cell[i, i]), value)
+            halves.append(value)
+        done.append(halves)
+    return done
 
 
 def factor_panels(works, outs, size):
     for p in range(0, size, PANEL):
         for work, out in zip(works, outs):
-            rows = jnp.concatenate(eliminate(work[p : p + PANEL, :], p), axis=0)
-            out[p : p + PANEL, :] = rows
+            tiles = [
+                (work[q : q + GROUP, :size], work[q : q + GROUP, size:])
+                for q in range(p, p + PANEL, GROUP)
+            ]
+            for g, (left, right) in enumerate(eliminate(tiles, p)):
+                at = p + g * GROUP
+                out[at : at + GROUP, :size] = left
+                out[at : at + GROUP, size:] = right
             if p + PANEL < size:
-                left = size - p - PANEL
+                rows = out[p : p + PANEL, :]
                 drop = mm(rows[:, :size], rows, ((0,), (0,)))
                 work[p + PANEL :, :] = work[p + PANEL :, :] - drop[p + PANEL :, :]
 
 
-def factors_kernel(gram_ref, seed_ref, basis_ref, tri_ref, rest, image, work_a, out_a, work_b, out_b):
+def factors_kernel(packed_ref, seed_ref, basis_ref, tri_ref, gram_ref, rest, image, work_a, out_a, work_b, out_b):
     size = seed_ref.shape[1]
-    total = gram_ref.shape[0]
+    total = seed_ref.shape[0]
+    for number, (i, j) in enumerate(upper_blocks(total // size)):
+        block = packed_ref[number * size : (number + 1) * size, :]
+        gram_ref[i * size : (i + 1) * size, j * size : (j + 1) * size] = block
+        if i != j:
+            gram_ref[j * size : (j + 1) * size, i * size : (i + 1) * size] = block.T
     row = lax.broadcasted_iota(jnp.int32, (size, size), 0)
     col = lax.broadcasted_iota(jnp.int32, (size, size), 1)
     eye = jnp.where(row == col, 1.0, 0.0).astype(jnp.float32)
@@ -108,7 +133,7 @@
             rest[...] = rest[...] - mm(strip, strip, ((0,), (0,)))
 
 
-def factors(gram, seed_subspace):
+def factors(packed, seed_subspace):
     total, size = seed_subspace.shape
     vmem = pl.BlockSpec(memory_space=pltpu.VMEM)
     return pl.pallas_call(
@@ -121,26 +146,246 @@
         out_specs=[vmem] * 2,
         scratch_shapes=[
             pltpu.VMEM((total, total), jnp.float32),
+            pltpu.VMEM((total, total), jnp.float32),
             pltpu.VMEM((total, size), jnp.float32),
         ]
         + [pltpu.VMEM((size, 2 * size), jnp.float32)] * 4,
         compiler_params=pltpu.CompilerParams(vmem_limit_bytes=32 * 1024 * 1024),
-    )(gram, seed_subspace)
+    )(packed, seed_subspace)
+
+
+MESH = pl.DeviceIdType.MESH
+
+
+def greet(peers):
+    barrier = pltpu.get_barrier_semaphore()
+    for peer in peers:
+        pl.semaphore_signal(barrier, inc=1, device_id=peer, device_id_type=MESH)
+    pl.semaphore_wait(barrier, len(peers))
+
+
+def send(src, dst, sems, slot, peer):
+    copy = pltpu.make_async_remote_copy(
+        src_ref=src,
+        dst_ref=dst,
+        send_sem=sems[0].at[slot],
+        recv_sem=sems[1].at[slot],
+        device_id=peer,
+        device_id_type=MESH,
+    )
+    copy.start()
+    return copy
+
+
+def gram_kernel(
+    reals, depth, chunks, field_ref, held_ref, out_ref, acc, packed,
+    from_core, half, from_real, quarter, from_depth, own_sem,
+    field_send, field_recv, sum_send, sum_recv, gather_send, gather_recv,
+):
+    r, cell = lax.axis_index("real"), lax.axis_index("cell")
+    z, c = cell // 2, cell % 2
+    cells, snaps, width = held_ref.shape[1:]
+    real_peers = [lax.rem(r + d, reals) for d in range(1, reals)]
+    depth_peers = [lax.rem(z + d, depth) for d in range(1, depth)]
+    to_core = {"real": r, "cell": z * 2 + 1 - c}
+    to_real = [{"real": q, "cell": cell} for q in real_peers]
+    to_depth = [{"real": r, "cell": q * 2 + c} for q in depth_peers]
+    greet([to_core] + to_real + to_depth)
+
+    step = cells // chunks
+    moves = []
+    for k in range(chunks):
+        own = pltpu.make_async_copy(
+            field_ref.at[pl.ds(k * step, step), pl.ds(r * snaps, snaps), :],
+            held_ref.at[r, pl.ds(k * step, step)],
+            own_sem.at[k],
+        )
+        own.start()
+        moves.append([own])
+        for d, (q, peer) in enumerate(zip(real_peers, to_real)):
+            moves[k].append(
+                send(
+                    field_ref.at[pl.ds(k * step, step), pl.ds(q * snaps, snaps), :],
+                    held_ref.at[r, pl.ds(k * step, step)],
+                    (field_send, field_recv),
+                    k * (reals - 1) + d,
+                    peer,
+                )
+            )
+    total_rows = cells * snaps * reals * depth * 2
+    for k in range(chunks):
+        moves[k][0].wait()
+        for copy in moves[k][1:]:
+            copy.wait_recv()
+        rows = jnp.concatenate(
+            [
+                held_ref[s, k * step : (k + 1) * step].reshape(step * snaps, width)
+                for s in range(reals)
+            ],
+            axis=1,
+        )
+        part = mm(rows, rows, ((0,), (0,)))
+        acc[...] = part if k == 0 else acc[...] + part
+    for k in range(chunks):
+        for copy in moves[k][1:]:
+            copy.wait_send()
+
+    blocks = upper_blocks(reals)
+    for number, (i, j) in enumerate(blocks):
+        packed[number * width : (number + 1) * width, :] = (
+            acc[i * width : (i + 1) * width, j * width : (j + 1) * width] / total_rows
+        )
+    used = len(blocks) * width
+    if packed.shape[0] > used:
+        packed[used:, :] = jnp.zeros((packed.shape[0] - used, width), jnp.float32)
+
+    sums = (sum_send, sum_recv)
+    h, q, e = half.shape[0], quarter.shape[0], from_depth.shape[1]
+    copy = send(packed.at[pl.ds((1 - c) * h, h)], from_core, sums, 0, to_core)
+    copy.wait()
+    half[...] = packed[pl.ds(pl.multiple_of(c * h, 8), h), :] + from_core[...]
+    copies = [
+        send(half.at[pl.ds(p * q, q)], from_real.at[d], sums, 1 + d, peer)
+        for d, (p, peer) in enumerate(zip(real_peers, to_real))
+    ]
+    for copy in copies:
+        copy.wait()
+    value = half[pl.ds(pl.multiple_of(r * q, 8), q), :]
+    for d in range(reals - 1):
+        value = value + from_real[d]
+    quarter[...] = value
+    copies = [
+        send(quarter.at[pl.ds(p * e, e)], from_depth.at[d], sums, reals + d, peer)
+        for d, (p, peer) in enumerate(zip(depth_peers, to_depth))
+    ]
+    for copy in copies:
+        copy.wait()
+    value = quarter[pl.ds(pl.multiple_of(z * e, 8), e), :]
+    for d in range(depth - 1):
+        value = value + from_depth[d]
+
+    gathers = (gather_send, gather_recv)
+    base = c * h + r * q
+    mine = pl.multiple_of(base + z * e, 8)
+    out_ref[pl.ds(mine, e), :] = value
+    for first, count, slot, peers in (
+        (mine, e, reals, to_depth),
+        (base, q, 1, to_real),
+        (c * h, h, 0, [to_core]),
+    ):
+        part = out_ref.at[pl.ds(first, count)]
+        copies = [send(part, part, gathers, slot + d, peer) for d, peer in enumerate(peers)]
+        for copy in copies:
+            copy.wait()
+
+
+def gathered_gram(field, reals, depth):
+    cells, snaps, width = field.shape
+    snaps //= reals
+    chunks = 4
+    used = len(upper_blocks(reals)) * width
+    e = -(-used // (2 * reals * depth * 8)) * 8
+    q = e * depth
+    h = q * reals
+    peers = reals + depth - 1
+    f32 = jnp.float32
+    dma = pltpu.SemaphoreType.DMA
+    vmem = pl.BlockSpec(memory_space=pltpu.VMEM)
+    return pl.pallas_call(
+        functools.partial(gram_kernel, reals, depth, chunks),
+        out_shape=(
+            jax.ShapeDtypeStruct((reals, cells, snaps, width), f32),
+            jax.ShapeDtypeStruct((2 * h, width), f32),
+        ),
+        in_specs=[pl.BlockSpec(memory_space=pl.ANY)],
+        out_specs=[vmem] * 2,
+        scratch_shapes=[
+            pltpu.VMEM((reals * width, reals * width), f32),
+            pltpu.VMEM((2 * h, width), f32),
+            pltpu.VMEM((h, width), f32),
+            pltpu.VMEM((h, width), f32),
+            pltpu.VMEM((reals - 1, q, width), f32),
+            pltpu.VMEM((q, width), f32),
+            pltpu.VMEM((depth - 1, e, width), f32),
+            dma((chunks,)),
+            dma((chunks * (reals - 1),)),
+            dma((chunks * (reals - 1),)),
+            dma((peers,)),
+            dma((peers,)),
+            dma((peers,)),
+            dma((peers,)),
+        ],
+        compiler_params=pltpu.CompilerParams(
+            collective_id=0, has_side_effects=True, vmem_limit_bytes=40 * 1024 * 1024
+        ),
+    )(field)
+
+
+def core_kernel(reals, held_ref, basis_ref, got_ref, sending, send_sem, recv_sem):
+    r, cell = lax.axis_index("real"), lax.axis_index("cell")
+    peers = [lax.rem(r + d, reals) for d in range(1, reals)]
+    places = [{"real": q, "cell": cell} for q in peers]
+    greet(places)
+    rows, width = held_ref.shape[1:]
+    ranks = got_ref.shape[1]
+    parts = 4
+    count = rows // parts
+    copies = []
+    for part in range(parts):
+        first = part * count
+        value = mm(held_ref[0, first : first + count, :], basis_ref[:width, :])
+        for s in range(1, reals):
+            value = value + mm(
+                held_ref[s, first : first + count, :], basis_ref[s * width : (s + 1) * width, :]
+            )
+        turned = value.T
+        for s in range(reals):
+            sending[s, :, first : first + count] = turned[s * ranks : (s + 1) * ranks, :]
+        lanes = pl.ds(first, count)
+        for d, (q, place) in enumerate(zip(peers, places)):
+            copies.append(
+                send(
+                    sending.at[q, :, lanes],
+                    got_ref.at[r, :, lanes],
+                    (send_sem, recv_sem),
+                    part * (reals - 1) + d,
+                    place,
+                )
+            )
+    got_ref[pl.ds(r, 1)] = sending[pl.ds(r, 1)]
+    for copy in copies:
+        copy.wait()
+
+
+def projected(held, basis, reals):
+    rows, width = held.shape[1:]
+    rank = basis.shape[1]
+    shape = (reals, rank // reals, rows)
+    vmem = pl.BlockSpec(memory_space=pltpu.VMEM)
+    return pl.pallas_call(
+        functools.partial(core_kernel, reals),
+        out_shape=jax.ShapeDtypeStruct(shape, jnp.float32),
+        in_specs=[vmem] * 2,
+        out_specs=vmem,
+        scratch_shapes=[
+            pltpu.VMEM(shape, jnp.float32),
+            pltpu.SemaphoreType.DMA((4 * (reals - 1),)),
+            pltpu.SemaphoreType.DMA((4 * (reals - 1),)),
+        ],
+        compiler_params=pltpu.CompilerParams(
+            collective_id=1, has_side_effects=True, vmem_limit_bytes=40 * 1024 * 1024
+        ),
+    )(held, basis)
 
 
 def local(soil_heat_field, seed_subspace):
-    permuted_array = lax.all_to_all(
-        soil_heat_field, "real", split_axis=1, concat_axis=2, tiled=True
-    )
-    flat = permuted_array.reshape(-1, permuted_array.shape[2])
-    total_rows = flat.shape[0] * lax.axis_size(("real", "cell"))
-    summed = lax.psum(mm(flat, flat, ((0,), (0,))) / total_rows, ("real", "cell"))
-    mode_factor, triangle = factors(summed, seed_subspace)
-    compressed = mm(flat, mode_factor).reshape(
-        permuted_array.shape[0], permuted_array.shape[1], -1
-    )
-    core_tensor = lax.all_to_all(compressed, "real", split_axis=2, concat_axis=1, tiled=True)
-    return (core_tensor, mode_factor, triangle)
+    reals, depth = lax.axis_size("real"), lax.axis_size("cell") // 2
+    held, packed = gathered_gram(soil_heat_field, reals, depth)
+    mode_factor, triangle = factors(packed, seed_subspace)
+    cells, snaps, width = held.shape[1:]
+    got = projected(held.reshape(reals, cells * snaps, width), mode_factor, reals)
+    core_tensor = got.reshape(reals, -1, cells, snaps).transpose(2, 0, 3, 1)
+    return (core_tensor.reshape(cells, reals * snaps, -1), mode_factor, triangle)
 
 
 def solution(mesh):

time: 354 us -> 139 us (0.39)
  waiting for transfers between devices: 130 us -> 0 us
  blocking collectives: 69 us -> 0 us
  Pallas kernels: 97.8 us -> 128 us
  matrix products: 14.6 us -> 0 us
  between operations: 14.3 us -> 0.67 us
  local copies, waits for them, and re-layouts: 21.6 us -> 9.84 us
  other arithmetic: 3.68 us -> 0 us
    psum x1 -> x0, waiting for transfers between devices: 130 us -> none  [local(): lax.psum(mm(flat, flat, ((0,), (0,))) / total_rows, ('real', 'cell'))]
    pallas_call x0 -> x2, Pallas kernels: none -> 92.2 us  [the longest x1 75.9 us: gathered_gram(): pl.pallas_call(functools.partial(gram_kernel, reals, depth, chunks), out_...]
    all_to_all x2 -> x0, blocking collectives: 69 us -> none  [the longest x1 53 us: local(): lax.all_to_all(soil_heat_field, 'real', split_axis=1, concat_axis=2, tile...]
    pallas_call x1, Pallas kernels: 97.8 us -> 36 us  [factors(): pl.pallas_call(factors_kernel, out_shape=(jax.ShapeDtypeStruct((total, si...]
    dot_general x2 -> x0, matrix products: 14.6 us -> none  [mm(): lax.dot_general(a, b, (dims, ((), ())), precision=HI, preferred_element_t...]
    all_to_all x4 -> x0, local copies, waits for them, and re-layouts: 9.11 us -> none  [the longest x3 6.41 us: local(): lax.all_to_all(compressed, 'real', split_axis=2, concat_axis=1, tiled=True)]
    unnamed x9 -> x6, local copies, waits for them, and re-layouts: 10.1 us -> 3.13 us
    all_to_all x1 -> x0, other arithmetic: 3.68 us -> none  [local(): lax.all_to_all(compressed, 'real', split_axis=2, concat_axis=1, tiled=True)]
  transfers between devices with their start and end apart: 1 -> 0, of which waited for: 1 -> 0; matrix products, arithmetic and copies ran while one was open for 0% -> 0% of each run, Pallas kernels for 0% -> 0%
where the time goes in v2:
time: 139 us
  Pallas kernels  128 us (92%)
  local copies, waits for them, and re-layouts  9.84 us (7%)
    pallas_call x1, Pallas kernels, gathered_gram(): pl.pallas_call(functools.partial(gram_kernel, reals, depth, chunks), out_...  75.9 us
    pallas_call x1, Pallas kernels, factors(): pl.pallas_call(factors_kernel, out_shape=(jax.ShapeDtypeStruct((total, si...  36 us
    pallas_call x1, Pallas kernels, projected(): pl.pallas_call(functools.partial(core_kernel, reals), out_shape=jax.Shape...  16.3 us
    reshape x1, local copies, waits for them, and re-layouts, local(): core_tensor.reshape(cells, reals * snaps, -1)  3.2 us
    unnamed x6, local copies, waits for them, and re-layouts  3.13 us

profile of v2, /device:TPU:0, one launch (start us, length us, event | category | flops | bytes accessed | tf_op | source)
XLA Modules:
  0.0 138.7 jit_solution(10923034392014849357)
XLA Ops:
  0.6 0.0 copy-start
  0.6 2.2 %copy-done = f32[32,256,128]{2,1,0:T(8,128)S(1)} copy-done((f32[32,256,128]{2,1,0:T(8,128)S(1)}, f32[32,256,128]{2,1,0:T(8,128)}, u32[]{:S(2)}) %copy-start) | copy-done | bytes 4194328
  2.8 0.0 copy-start.1
  2.8 75.9 %shard_map.49 = (f32[4,32,64,128]{3,2,1,0:T(8,128)S(1)}, f32[1280,128]{1,0:T(8,128)S(1)}) custom-call(f32[32,256,128]{2,1,0:T(8,128)S(1)} %copy-done), custom_call_target="tpu_custom_call" | custom-call | tf_op jit(solution)/shard_map/pallas_call | solution.py:294
  78.7 0.0 copy-done.1
  78.7 36.0 %shard_map.50 = (f32[512,128]{1,0:T(8,128)}, f32[512,512]{1,0:T(8,128)}) custom-call(f32[1280,128]{1,0:T(8,128)S(1)} %get-tuple-element.8.packed_ref, f32[512,128]{1,0:T(8,128)S(1)} %copy-done.1), custom_call_target="tpu_custom_call" | custom-call | tf_op jit(solution)/shard_map/pallas_call | solution.py:139
  114.7 0.0 copy-start.2
  114.7 0.9 copy-done.2
  115.7 16.3 %shard_map.51 = f32[4,32,2048]{2,1,0:T(8,128)S(1)} custom-call(f32[4,2048,128]{2,1,0:T(8,128)S(1)} %bitcast.4, f32[512,128]{1,0:T(8,128)S(1)} %copy-done.2), custom_call_target="tpu_custom_call" | custom-call | tf_op jit(solution)/shard_map/pallas_call | solution.py:365
  132.0 0.8 reshape.16
  132.8 2.7 %copy.5 = f32[32,4,64,32]{2,1,3,0:T(4,128)} copy(f32[32,4,64,32]{2,0,3,1:T(8,128)S(1)} %bitcast.5) | data formatting | bytes 2097152 | tf_op jit(solution)/shard_map/transpose | solution.py:387
  135.5 3.2 %reshape.17 = f32[32,256,32]{1,2,0:T(8,128)} reshape(f32[32,4,64,32]{2,1,3,0:T(4,128)} %copy.5) | data formatting | bytes 2097152 | tf_op jit(solution)/shard_map/reshape | solution.py:388
Async XLA Ops:
  0.6 2.2 %copy-start = (f32[32,256,128]{2,1,0:T(8,128)S(1)}, f32[32,256,128]{2,1,0:T(8,128)}, u32[]{:S(2)}) copy-start(f32[32,256,128]{2,1,0:T(8,128)} %field_ref.1) | copy-start | bytes 12582916
  2.8 75.9 %copy-start.1 = (f32[512,128]{1,0:T(8,128)S(1)}, f32[512,128]{1,0:T(8,128)}, u32[]{:S(2)}) copy-start(f32[512,128]{1,0:T(8,128)} %seed_ref.1) | copy-start | bytes 786436
  114.7 0.9 copy-start.2

commit v3 on v2

--- a/solution.py
+++ b/solution.py
@@ -24,6 +24,11 @@
 
 def spread(tile, lane):
     return jnp.broadcast_to(tile[:, lane : lane + 1], tile.shape)
+
+
+def reciprocal(x):
+    guess = pl.reciprocal(x, approx=True)
+    return guess * (2.0 - x * guess)
 
 
 def eliminate(tiles, first_lane):
@@ -43,7 +48,7 @@
         }
         cols = [[spread(t[0], lane + k) for t in rest] for k in range(GROUP)]
         for i in range(GROUP):
-            inverse = 1.0 / cell[i, i]
+            inverse = reciprocal(cell[i, i])
             for k in range(i + 1, GROUP):
                 factor = cell[i, k] * inverse
                 for q in range(k, GROUP):
@@ -55,12 +60,13 @@
                 tuple(x - c * y for x, y in zip(t, scaled)) for t, c in zip(rest, cols[i])
             ]
         tiles = tiles[: g + 1] + rest
-        halves = []
-        for h in range(2):
-            value = rows[0][h] * lax.rsqrt(cell[0, 0])
-            for i in range(1, GROUP):
-                value = jnp.where(sub == i, rows[i][h] * lax.rsqrt(cell[i, i]), value)
-            halves.append(value)
+        pivots, halves = cell[0, 0], rows[0]
+        for i in range(1, GROUP):
+            here = sub == i
+            pivots = jnp.where(here, cell[i, i], pivots)
+            halves = [jnp.where(here, x, y) for x, y in zip(rows[i], halves)]
+        scale = lax.rsqrt(pivots)
+        halves = [x * scale for x in halves]
         done.append(halves)
     return done
 
@@ -82,7 +88,7 @@
                 work[p + PANEL :, :] = work[p + PANEL :, :] - drop[p + PANEL :, :]
 
 
-def factors_kernel(packed_ref, seed_ref, basis_ref, tri_ref, gram_ref, rest, image, work_a, out_a, work_b, out_b):
+def factors_kernel(packed_ref, seed_ref, basis_ref, tri_ref, last_ref, gram_ref, rest, image, work_a, out_a, work_b, out_b):
     size = seed_ref.shape[1]
     total = seed_ref.shape[0]
     for number, (i, j) in enumerate(upper_blocks(total // size)):
@@ -125,12 +131,13 @@
 
     blocks = total // size
     lax.fori_loop(0, ITERS, step, 0)
-    for block in range(ITERS, blocks):
+    for block in range(ITERS, blocks - 1):
         triangle_start(block)
         factor_panels([work_b], [out_b], size)
         strip = triangle_end(block)
-        if block + 1 < blocks:
-            rest[...] = rest[...] - mm(strip, strip, ((0,), (0,)))
+        rest[...] = rest[...] - mm(strip, strip, ((0,), (0,)))
+    tri_ref[total - size :, :] = jnp.zeros((size, total), jnp.float32)
+    last_ref[...] = rest[total - size :, total - size :]
 
 
 def factors(packed, seed_subspace):
@@ -141,9 +148,10 @@
         out_shape=(
             jax.ShapeDtypeStruct((total, size), jnp.float32),
             jax.ShapeDtypeStruct((total, total), jnp.float32),
+            jax.ShapeDtypeStruct((size, size), jnp.float32),
         ),
         in_specs=[vmem] * 2,
-        out_specs=[vmem] * 2,
+        out_specs=[vmem] * 3,
         scratch_shapes=[
             pltpu.VMEM((total, total), jnp.float32),
             pltpu.VMEM((total, total), jnp.float32),
@@ -282,7 +290,7 @@
 def gathered_gram(field, reals, depth):
     cells, snaps, width = field.shape
     snaps //= reals
-    chunks = 4
+    chunks = 8
     used = len(upper_blocks(reals)) * width
     e = -(-used // (2 * reals * depth * 8)) * 8
     q = e * depth
@@ -316,12 +324,15 @@
             dma((peers,)),
         ],
         compiler_params=pltpu.CompilerParams(
-            collective_id=0, has_side_effects=True, vmem_limit_bytes=40 * 1024 * 1024
+            collective_id=0, has_side_effects=True, vmem_limit_bytes=60 * 1024 * 1024
         ),
     )(field)
 
 
-def core_kernel(reals, held_ref, basis_ref, got_ref, sending, send_sem, recv_sem):
+def core_kernel(
+    reals, held_ref, basis_ref, last_ref, got_ref, corner_ref,
+    sending, work, out, send_sem, recv_sem,
+):
     r, cell = lax.axis_index("real"), lax.axis_index("cell")
     peers = [lax.rem(r + d, reals) for d in range(1, reals)]
     places = [{"real": q, "cell": cell} for q in peers]
@@ -353,39 +364,75 @@
                 )
             )
     got_ref[pl.ds(r, 1)] = sending[pl.ds(r, 1)]
+    size = last_ref.shape[0]
+    row = lax.broadcasted_iota(jnp.int32, (size, size), 0)
+    col = lax.broadcasted_iota(jnp.int32, (size, size), 1)
+    work[:, :size] = last_ref[...]
+    work[:, size:] = jnp.where(row == col, 1.0, 0.0).astype(jnp.float32)
+    factor_panels([work], [out], size)
+    corner_ref[...] = jnp.where(col >= row, out[:, :size], 0.0)
     for copy in copies:
         copy.wait()
 
 
-def projected(held, basis, reals):
+def projected(held, basis, last, reals):
     rows, width = held.shape[1:]
     rank = basis.shape[1]
+    size = last.shape[0]
     shape = (reals, rank // reals, rows)
     vmem = pl.BlockSpec(memory_space=pltpu.VMEM)
     return pl.pallas_call(
         functools.partial(core_kernel, reals),
-        out_shape=jax.ShapeDtypeStruct(shape, jnp.float32),
-        in_specs=[vmem] * 2,
-        out_specs=vmem,
+        out_shape=(
+            jax.ShapeDtypeStruct(shape, jnp.float32),
+            jax.ShapeDtypeStruct(last.shape, jnp.float32),
+        ),
+        in_specs=[vmem] * 3,
+        out_specs=[vmem] * 2,
         scratch_shapes=[
             pltpu.VMEM(shape, jnp.float32),
+            pltpu.VMEM((size, 2 * size), jnp.float32),
+            pltpu.VMEM((size, 2 * size), jnp.float32),
             pltpu.SemaphoreType.DMA((4 * (reals - 1),)),
             pltpu.SemaphoreType.DMA((4 * (reals - 1),)),
         ],
         compiler_params=pltpu.CompilerParams(
             collective_id=1, has_side_effects=True, vmem_limit_bytes=40 * 1024 * 1024
         ),
-    )(held, basis)
+    )(held, basis, last)
+
+
+def place_kernel(snaps, got_ref, core_ref):
+    reals = got_ref.shape[0]
+    for cell in range(core_ref.shape[0]):
+        lanes = slice(cell * snaps, (cell + 1) * snaps)
+        core_ref[cell] = jnp.concatenate([got_ref[s, :, lanes] for s in range(reals)], axis=1)
+
+
+def placed(got, snaps):
+    reals, ranks, rows = got.shape
+    cells, steps = rows // snaps, 2
+    return pl.pallas_call(
+        functools.partial(place_kernel, snaps),
+        grid=(steps,),
+        out_shape=jax.ShapeDtypeStruct((cells, ranks, reals * snaps), jnp.float32),
+        in_specs=[pl.BlockSpec((reals, ranks, rows // steps), lambda i: (0, 0, i))],
+        out_specs=pl.BlockSpec((cells // steps, ranks, reals * snaps), lambda i: (i, 0, 0)),
+        compiler_params=pltpu.CompilerParams(vmem_limit_bytes=32 * 1024 * 1024),
+    )(got)
 
 
 def local(soil_heat_field, seed_subspace):
     reals, depth = lax.axis_size("real"), lax.axis_size("cell") // 2
     held, packed = gathered_gram(soil_heat_field, reals, depth)
-    mode_factor, triangle = factors(packed, seed_subspace)
+    mode_factor, triangle, last = factors(packed, seed_subspace)
     cells, snaps, width = held.shape[1:]
-    got = projected(held.reshape(reals, cells * snaps, width), mode_factor, reals)
-    core_tensor = got.reshape(reals, -1, cells, snaps).transpose(2, 0, 3, 1)
-    return (core_tensor.reshape(cells, reals * snaps, -1), mode_factor, triangle)
+    rows = held.reshape(reals, cells * snaps, width)
+    got, corner = projected(rows, mode_factor, last, reals)
+    core_tensor = placed(got, snaps).transpose(0, 2, 1)
+    first = triangle.shape[0] - corner.shape[0]
+    triangle = lax.dynamic_update_slice(triangle, corner, (first, first))
+    return (core_tensor, mode_factor, triangle)
 
 
 def solution(mesh):

time: 139 us -> 134 us (0.964)
  local copies, waits for them, and re-layouts: 9.84 us -> 4.86 us
    reshape x2 -> x0, local copies, waits for them, and re-layouts: 4.03 us -> none  [the longest x1 3.2 us: local(): core_tensor.reshape(cells, reals * snaps, -1)]
    pallas_call x1, Pallas kernels: 36 us -> 32.8 us  [factors(): pl.pallas_call(factors_kernel, out_shape=(jax.ShapeDtypeStruct((total, si...]
    transpose x1 -> x0, local copies, waits for them, and re-layouts: 2.68 us -> none  [local(): core_tensor = got.reshape(reals, -1, cells, snaps).transpose(2, 0, 3, 1)]
    pallas_call x1, Pallas kernels: 75.9 us -> 77.6 us  [gathered_gram(): pl.pallas_call(functools.partial(gram_kernel, reals, depth, chunks), out_...]
    pallas_call x1 -> x2, Pallas kernels: 16.3 us -> 17.5 us  [the longest x1 16.2 us: projected(): pl.pallas_call(functools.partial(core_kernel, reals), out_shape=(jax.Shap...]
    unnamed x6 -> x8, local copies, waits for them, and re-layouts: 3.13 us -> 4.22 us
where the time goes in v3:
time: 134 us; the launch traced here: 133 us
  Pallas kernels  128 us (96%)
  local copies, waits for them, and re-layouts  4.86 us (4%)
    pallas_call x1, Pallas kernels, gathered_gram(): pl.pallas_call(functools.partial(gram_kernel, reals, depth, chunks), out_...  77.6 us
    pallas_call x1, Pallas kernels, factors(): pl.pallas_call(factors_kernel, out_shape=(jax.ShapeDtypeStruct((total, si...  32.8 us
    pallas_call x1, Pallas kernels, projected(): pl.pallas_call(functools.partial(core_kernel, reals), out_shape=(jax.Shap...  16.2 us
    unnamed x8, local copies, waits for them, and re-layouts  4.22 us

profile of v3, /device:TPU:0, one launch (start us, length us, event | category | flops | bytes accessed | tf_op | source)
XLA Modules:
  0.0 133.4 jit_solution(15442262485848494580)
XLA Ops:
  0.6 0.0 copy-start.2
  0.6 77.6 %shard_map.49 = (f32[4,32,64,128]{3,2,1,0:T(8,128)}, f32[1280,128]{1,0:T(8,128)}) custom-call(f32[32,256,128]{2,1,0:T(8,128)} %field_ref.1), custom_call_target="tpu_custom_call" | custom-call | tf_op jit(solution)/shard_map/pallas_call | solution.py:302
  78.3 0.0 copy-done.2
  78.3 0.0 copy-start.1
  78.3 1.1 copy-done.1
  79.4 32.8 %shard_map.50 = (f32[512,128]{1,0:T(8,128)}, f32[512,512]{1,0:T(8,128)}, f32[128,128]{1,0:T(8,128)S(1)}) custom-call(f32[1280,128]{1,0:T(8,128)S(1)} %copy-done.1, f32[512,128]{1,0:T(8,128)S(1)} %copy-done.2), custom_call_target="tpu_custom_call" | custom-call | tf_op jit(solution)/shard_map/pallas_call | solution.py:146
  112.1 0.0 copy-start
  112.1 2.2 %copy-done = f32[4,32,64,128]{3,2,1,0:T(8,128)S(1)} copy-done((f32[4,32,64,128]{3,2,1,0:T(8,128)S(1)}, f32[4,32,64,128]{3,2,1,0:T(8,128)}, u32[]{:S(2)}) %copy-start) | copy-done | bytes 4194328
  114.3 0.0 copy-start.3
  114.3 0.9 copy-done.3
  115.3 16.2 %shard_map.51 = (f32[4,32,2048]{2,1,0:T(8,128)S(1)}, f32[128,128]{1,0:T(8,128)S(1)}) custom-call(f32[4,2048,128]{2,1,0:T(8,128)S(1)} %bitcast.2, f32[512,128]{1,0:T(8,128)S(1)} %copy-done.3, f32[128,128]{1,0:T(8,128)S(1)} %get-tuple-element.13.last_ref), custom_call_target="tpu_custom_call" | custom-call | tf_op jit(solution)/shard_map/pallas_call | solution.py:384
  131.5 1.3 shard_map.52
  132.8 0.6 constant_dynamic-update-slice_fusion
Async XLA Ops:
  0.6 77.6 %copy-start.2 = (f32[512,128]{1,0:T(8,128)S(1)}, f32[512,128]{1,0:T(8,128)}, u32[]{:S(2)}) copy-start(f32[512,128]{1,0:T(8,128)} %seed_ref.1) | copy-start | bytes 786436
  78.3 1.1 copy-start.1
  112.1 2.2 %copy-start = (f32[4,32,64,128]{3,2,1,0:T(8,128)S(1)}, f32[4,32,64,128]{3,2,1,0:T(8,128)}, u32[]{:S(2)}) copy-start(f32[4,32,64,128]{3,2,1,0:T(8,128)} %get-tuple-element.10) | copy-start | bytes 12582916
  114.3 0.9 copy-start.3

commit v4 on v3

--- a/solution.py
+++ b/solution.py
@@ -88,28 +88,30 @@
                 work[p + PANEL :, :] = work[p + PANEL :, :] - drop[p + PANEL :, :]
 
 
-def factors_kernel(packed_ref, seed_ref, basis_ref, tri_ref, last_ref, gram_ref, rest, image, work_a, out_a, work_b, out_b):
-    size = seed_ref.shape[1]
-    total = seed_ref.shape[0]
-    for number, (i, j) in enumerate(upper_blocks(total // size)):
+def unpack(packed_ref, gram_ref):
+    size = packed_ref.shape[1]
+    for number, (i, j) in enumerate(upper_blocks(gram_ref.shape[0] // size)):
         block = packed_ref[number * size : (number + 1) * size, :]
         gram_ref[i * size : (i + 1) * size, j * size : (j + 1) * size] = block
         if i != j:
             gram_ref[j * size : (j + 1) * size, i * size : (i + 1) * size] = block.T
+
+
+def positions(size):
     row = lax.broadcasted_iota(jnp.int32, (size, size), 0)
-    col = lax.broadcasted_iota(jnp.int32, (size, size), 1)
-    eye = jnp.where(row == col, 1.0, 0.0).astype(jnp.float32)
-    rest[...] = gram_ref[...]
-    basis_ref[...] = seed_ref[...]
-
-    def triangle_start(block):
+    return row, lax.broadcasted_iota(jnp.int32, (size, size), 1)
+
+
+def triangle_rows(tri_ref, rest, work, out):
+    total, size = rest.shape[0], work.shape[0]
+    row, col = positions(size)
+
+    def block_rows(block):
         at = pl.multiple_of(block * size, size)
-        work_b[:, :size] = rest[pl.ds(at, size), pl.ds(at, size)]
-        work_b[:, size:] = eye
-
-    def triangle_end(block):
-        at = pl.multiple_of(block * size, size)
-        inverse = jnp.where(row >= col, out_b[:, size:], 0.0)
+        work[:, :size] = rest[pl.ds(at, size), pl.ds(at, size)]
+        work[:, size:] = jnp.where(row == col, 1.0, 0.0).astype(jnp.float32)
+        factor_panels([work], [out], size)
+        inverse = jnp.where(row >= col, out[:, size:], 0.0)
         strip = mm(inverse, rest[pl.ds(at, size), :])
         rows = at + lax.broadcasted_iota(jnp.int32, (size, total), 0)
         cols = lax.broadcasted_iota(jnp.int32, (size, total), 1)
@@ -117,47 +119,48 @@
         tri_ref[pl.ds(at, size), :] = strip
         return strip
 
+    def step(block, carry):
+        strip = block_rows(block)
+        rest[...] = rest[...] - mm(strip, strip, ((0,), (0,)))
+        return carry
+
+    blocks = total // size
+    lax.fori_loop(0, blocks - 1, step, 0)
+    block_rows(blocks - 1)
+
+
+def basis_kernel(packed_ref, seed_ref, basis_ref, gram_ref, image, work, out):
+    size = seed_ref.shape[1]
+    row, col = positions(size)
+    unpack(packed_ref, gram_ref)
+    basis_ref[...] = seed_ref[...]
+
     def step(index, carry):
         image[...] = mm(gram_ref[...], basis_ref[...])
-        work_a[:, :size] = mm(image[...], image[...], ((0,), (0,)))
-        work_a[:, size:] = eye
-        triangle_start(index)
-        factor_panels([work_a, work_b], [out_a, out_b], size)
-        inverse = jnp.where(row >= col, out_a[:, size:], 0.0)
+        work[:, :size] = mm(image[...], image[...], ((0,), (0,)))
+        work[:, size:] = jnp.where(row == col, 1.0, 0.0).astype(jnp.float32)
+        factor_panels([work], [out], size)
+        inverse = jnp.where(row >= col, out[:, size:], 0.0)
         basis_ref[...] = mm(image[...], inverse, ((1,), (1,)))
-        strip = triangle_end(index)
-        rest[...] = rest[...] - mm(strip, strip, ((0,), (0,)))
         return carry
 
-    blocks = total // size
     lax.fori_loop(0, ITERS, step, 0)
-    for block in range(ITERS, blocks - 1):
-        triangle_start(block)
-        factor_panels([work_b], [out_b], size)
-        strip = triangle_end(block)
-        rest[...] = rest[...] - mm(strip, strip, ((0,), (0,)))
-    tri_ref[total - size :, :] = jnp.zeros((size, total), jnp.float32)
-    last_ref[...] = rest[total - size :, total - size :]
-
-
-def factors(packed, seed_subspace):
+
+
+def iterated(packed, seed_subspace):
     total, size = seed_subspace.shape
     vmem = pl.BlockSpec(memory_space=pltpu.VMEM)
     return pl.pallas_call(
-        factors_kernel,
-        out_shape=(
-            jax.ShapeDtypeStruct((total, size), jnp.float32),
-            jax.ShapeDtypeStruct((total, total), jnp.float32),
-            jax.ShapeDtypeStruct((size, size), jnp.float32),
-        ),
+        basis_kernel,
+        out_shape=jax.ShapeDtypeStruct((total, size), jnp.float32),
         in_specs=[vmem] * 2,
-        out_specs=[vmem] * 3,
+        out_specs=vmem,
         scratch_shapes=[
             pltpu.VMEM((total, total), jnp.float32),
-            pltpu.VMEM((total, total), jnp.float32),
             pltpu.VMEM((total, size), jnp.float32),
-        ]
-        + [pltpu.VMEM((size, 2 * size), jnp.float32)] * 4,
+            pltpu.VMEM((size, 2 * size), jnp.float32),
+            pltpu.VMEM((size, 2 * size), jnp.float32),
+        ],
         compiler_params=pltpu.CompilerParams(vmem_limit_bytes=32 * 1024 * 1024),
     )(packed, seed_subspace)
 
@@ -186,8 +189,8 @@
 
 
 def gram_kernel(
-    reals, depth, chunks, field_ref, held_ref, out_ref, acc, packed,
-    from_core, half, from_real, quarter, from_depth, own_sem,
+    reals, depth, chunks, field_ref, stored_ref, out_ref, held_ref, acc, packed,
+    from_core, half, from_real, quarter, from_depth, own_sem, store_sem,
     field_send, field_recv, sum_send, sum_recv, gather_send, gather_recv,
 ):
     r, cell = lax.axis_index("real"), lax.axis_index("cell")
@@ -221,10 +224,18 @@
                 )
             )
     total_rows = cells * snaps * reals * depth * 2
+    stores = []
     for k in range(chunks):
         moves[k][0].wait()
         for copy in moves[k][1:]:
             copy.wait_recv()
+        store = pltpu.make_async_copy(
+            held_ref.at[:, pl.ds(k * step, step)],
+            stored_ref.at[:, pl.ds(k * step, step)],
+            store_sem.at[k],
+        )
+        store.start()
+        stores.append(store)
         rows = jnp.concatenate(
             [
                 held_ref[s, k * step : (k + 1) * step].reshape(step * snaps, width)
@@ -285,6 +296,8 @@
         copies = [send(part, part, gathers, slot + d, peer) for d, peer in enumerate(peers)]
         for copy in copies:
             copy.wait()
+    for store in stores:
+        store.wait()
 
 
 def gathered_gram(field, reals, depth):
@@ -306,8 +319,9 @@
             jax.ShapeDtypeStruct((2 * h, width), f32),
         ),
         in_specs=[pl.BlockSpec(memory_space=pl.ANY)],
-        out_specs=[vmem] * 2,
+        out_specs=[pl.BlockSpec(memory_space=pl.ANY), vmem],
         scratch_shapes=[
+            pltpu.VMEM((reals, cells, snaps, width), f32),
             pltpu.VMEM((reals * width, reals * width), f32),
             pltpu.VMEM((2 * h, width), f32),
             pltpu.VMEM((h, width), f32),
@@ -315,6 +329,7 @@
             pltpu.VMEM((reals - 1, q, width), f32),
             pltpu.VMEM((q, width), f32),
             pltpu.VMEM((depth - 1, e, width), f32),
+            dma((chunks,)),
             dma((chunks,)),
             dma((chunks * (reals - 1),)),
             dma((chunks * (reals - 1),)),
@@ -330,20 +345,28 @@
 
 
 def core_kernel(
-    reals, held_ref, basis_ref, last_ref, got_ref, corner_ref,
-    sending, work, out, send_sem, recv_sem,
+    reals, parts, stored_ref, basis_ref, packed_ref, got_ref, tri_ref,
+    held_ref, sending, rest, work, out, load_sem, send_sem, recv_sem,
 ):
     r, cell = lax.axis_index("real"), lax.axis_index("cell")
+    rows, width = stored_ref.shape[1:]
+    count = rows // parts
+    loads = []
+    for part in range(parts):
+        place = pl.ds(part * count, count)
+        load = pltpu.make_async_copy(
+            stored_ref.at[:, place], held_ref.at[:, place], load_sem.at[part]
+        )
+        load.start()
+        loads.append(load)
     peers = [lax.rem(r + d, reals) for d in range(1, reals)]
     places = [{"real": q, "cell": cell} for q in peers]
     greet(places)
-    rows, width = held_ref.shape[1:]
     ranks = got_ref.shape[1]
-    parts = 4
-    count = rows // parts
     copies = []
     for part in range(parts):
         first = part * count
+        loads[part].wait()
         value = mm(held_ref[0, first : first + count, :], basis_ref[:width, :])
         for s in range(1, reals):
             value = value + mm(
@@ -364,42 +387,41 @@
                 )
             )
     got_ref[pl.ds(r, 1)] = sending[pl.ds(r, 1)]
-    size = last_ref.shape[0]
-    row = lax.broadcasted_iota(jnp.int32, (size, size), 0)
-    col = lax.broadcasted_iota(jnp.int32, (size, size), 1)
-    work[:, :size] = last_ref[...]
-    work[:, size:] = jnp.where(row == col, 1.0, 0.0).astype(jnp.float32)
-    factor_panels([work], [out], size)
-    corner_ref[...] = jnp.where(col >= row, out[:, :size], 0.0)
+    unpack(packed_ref, rest)
+    triangle_rows(tri_ref, rest, work, out)
     for copy in copies:
         copy.wait()
 
 
-def projected(held, basis, last, reals):
-    rows, width = held.shape[1:]
-    rank = basis.shape[1]
-    size = last.shape[0]
+def projected(stored, basis, packed, reals):
+    rows, width = stored.shape[1:]
+    total, rank = basis.shape
     shape = (reals, rank // reals, rows)
+    parts = 4
+    dma = pltpu.SemaphoreType.DMA
     vmem = pl.BlockSpec(memory_space=pltpu.VMEM)
     return pl.pallas_call(
-        functools.partial(core_kernel, reals),
+        functools.partial(core_kernel, reals, parts),
         out_shape=(
             jax.ShapeDtypeStruct(shape, jnp.float32),
-            jax.ShapeDtypeStruct(last.shape, jnp.float32),
+            jax.ShapeDtypeStruct((total, total), jnp.float32),
         ),
-        in_specs=[vmem] * 3,
+        in_specs=[pl.BlockSpec(memory_space=pl.ANY), vmem, vmem],
         out_specs=[vmem] * 2,
         scratch_shapes=[
+            pltpu.VMEM(stored.shape, jnp.float32),
             pltpu.VMEM(shape, jnp.float32),
-            pltpu.VMEM((size, 2 * size), jnp.float32),
-            pltpu.VMEM((size, 2 * size), jnp.float32),
-            pltpu.SemaphoreType.DMA((4 * (reals - 1),)),
-            pltpu.SemaphoreType.DMA((4 * (reals - 1),)),
+            pltpu.VMEM((total, total), jnp.float32),
+            pltpu.VMEM((width, 2 * width), jnp.float32),
+            pltpu.VMEM((width, 2 * width), jnp.float32),
+            dma((parts,)),
+            dma((parts * (reals - 1),)),
+            dma((parts * (reals - 1),)),
         ],
         compiler_params=pltpu.CompilerParams(
-            collective_id=1, has_side_effects=True, vmem_limit_bytes=40 * 1024 * 1024
+            collective_id=1, has_side_effects=True, vmem_limit_bytes=60 * 1024 * 1024
         ),
-    )(held, basis, last)
+    )(stored, basis, packed)
 
 
 def place_kernel(snaps, got_ref, core_ref):
@@ -424,14 +446,12 @@
 
 def local(soil_heat_field, seed_subspace):
     reals, depth = lax.axis_size("real"), lax.axis_size("cell") // 2
-    held, packed = gathered_gram(soil_heat_field, reals, depth)
-    mode_factor, triangle, last = factors(packed, seed_subspace)
-    cells, snaps, width = held.shape[1:]
-    rows = held.reshape(reals, cells * snaps, width)
-    got, corner = projected(rows, mode_factor, last, reals)
+    stored, packed = gathered_gram(soil_heat_field, reals, depth)
+    mode_factor = iterated(packed, seed_subspace)
+    cells, snaps, width = stored.shape[1:]
+    rows = stored.reshape(reals, cells * snaps, width)
+    got, triangle = projected(rows, mode_factor, packed, reals)
     core_tensor = placed(got, snaps).transpose(0, 2, 1)
-    first = triangle.shape[0] - corner.shape[0]
-    triangle = lax.dynamic_update_slice(triangle, corner, (first, first))
     return (core_tensor, mode_factor, triangle)
 
 

time: 134 us -> 143 us (1.067)
  Pallas kernels: 128 us -> 137 us
    pallas_call x2, Pallas kernels: 49 us -> 59.4 us  [the longest x1 35.9 us: projected(): pl.pallas_call(functools.partial(core_kernel, reals, parts), out_shape=(j...]
    unnamed x8 -> x7, local copies, waits for them, and re-layouts: 4.22 us -> 4.56 us
where the time goes in v4:
time: 143 us; the launch traced here: 142 us
  Pallas kernels  137 us (96%)
  local copies, waits for them, and re-layouts  4.56 us (3%)
    pallas_call x1, Pallas kernels, gathered_gram(): pl.pallas_call(functools.partial(gram_kernel, reals, depth, chunks), out_...  76.4 us
    pallas_call x1, Pallas kernels, projected(): pl.pallas_call(functools.partial(core_kernel, reals, parts), out_shape=(j...  35.9 us
    pallas_call x1, Pallas kernels, iterated(): pl.pallas_call(basis_kernel, out_shape=jax.ShapeDtypeStruct((total, size)...  23.5 us
    unnamed x7, local copies, waits for them, and re-layouts  4.56 us

profile of v4, /device:TPU:0, one launch (start us, length us, event | category | flops | bytes accessed | tf_op | source)
XLA Modules:
  0.0 142.3 jit_solution(7863232734804292623)
XLA Ops:
  0.6 0.0 copy-start.2
  0.6 76.4 %shard_map.49 = (f32[4,32,64,128]{3,2,1,0:T(8,128)}, f32[1280,128]{1,0:T(8,128)}) custom-call(f32[32,256,128]{2,1,0:T(8,128)} %field_ref.1), custom_call_target="tpu_custom_call" | custom-call | tf_op jit(solution)/shard_map/pallas_call | solution.py:315
  77.0 0.0 copy-done.2
  77.0 0.0 copy-start
  77.0 1.1 copy-done
  78.1 23.5 %shard_map.50.basis_ref = f32[512,128]{1,0:T(8,128)} custom-call(f32[1280,128]{1,0:T(8,128)S(1)} %copy-done, f32[512,128]{1,0:T(8,128)S(1)} %copy-done.2), custom_call_target="tpu_custom_call" | custom-call | tf_op jit(solution)/shard_map/pallas_call | solution.py:153
  101.6 35.9 %shard_map.51 = (f32[4,32,2048]{2,1,0:T(8,128)}, f32[512,512]{1,0:T(8,128)}) custom-call(f32[4,2048,128]{2,1,0:T(8,128)} %bitcast.2, f32[512,128]{1,0:T(8,128)} %shard_map.50.basis_ref, f32[1280,128]{1,0:T(8,128)} %get-tuple-element.8.packed_ref), custom_call_target="tpu_custom_call" | custom-call | tf_op jit(solution)/shard_map/pallas_call | solution.py:403
  137.5 0.0 copy-start.1
  137.5 1.2 copy-done.1
  138.7 1.3 shard_map.52
  140.0 2.3 %copy.6 = f32[512,512]{1,0:T(8,128)} copy(f32[512,512]{1,0:T(8,128)} %get-tuple-element.16) | data formatting | bytes 2097152
Async XLA Ops:
  0.6 76.4 %copy-start.2 = (f32[512,128]{1,0:T(8,128)S(1)}, f32[512,128]{1,0:T(8,128)}, u32[]{:S(2)}) copy-start(f32[512,128]{1,0:T(8,128)} %seed_ref.1) | copy-start | bytes 786436
  77.0 1.1 copy-start
  137.5 1.2 copy-start.1

commit v5 on v3

--- a/solution.py
+++ b/solution.py
@@ -186,8 +186,8 @@
 
 
 def gram_kernel(
-    reals, depth, chunks, field_ref, held_ref, out_ref, acc, packed,
-    from_core, half, from_real, quarter, from_depth, own_sem,
+    reals, depth, chunks, field_ref, stored_ref, out_ref, held_ref, acc, packed,
+    from_core, half, from_real, quarter, from_depth, own_sem, store_sem,
     field_send, field_recv, sum_send, sum_recv, gather_send, gather_recv,
 ):
     r, cell = lax.axis_index("real"), lax.axis_index("cell")
@@ -221,10 +221,18 @@
                 )
             )
     total_rows = cells * snaps * reals * depth * 2
+    stores = []
     for k in range(chunks):
         moves[k][0].wait()
         for copy in moves[k][1:]:
             copy.wait_recv()
+        store = pltpu.make_async_copy(
+            held_ref.at[:, pl.ds(k * step, step)],
+            stored_ref.at[:, pl.ds(k * step, step)],
+            store_sem.at[k],
+        )
+        store.start()
+        stores.append(store)
         rows = jnp.concatenate(
             [
                 held_ref[s, k * step : (k + 1) * step].reshape(step * snaps, width)
@@ -285,6 +293,8 @@
         copies = [send(part, part, gathers, slot + d, peer) for d, peer in enumerate(peers)]
         for copy in copies:
             copy.wait()
+    for store in stores:
+        store.wait()
 
 
 def gathered_gram(field, reals, depth):
@@ -306,8 +316,9 @@
             jax.ShapeDtypeStruct((2 * h, width), f32),
         ),
         in_specs=[pl.BlockSpec(memory_space=pl.ANY)],
-        out_specs=[vmem] * 2,
+        out_specs=[pl.BlockSpec(memory_space=pl.ANY), vmem],
         scratch_shapes=[
+            pltpu.VMEM((reals, cells, snaps, width), f32),
             pltpu.VMEM((reals * width, reals * width), f32),
             pltpu.VMEM((2 * h, width), f32),
             pltpu.VMEM((h, width), f32),
@@ -315,6 +326,7 @@
             pltpu.VMEM((reals - 1, q, width), f32),
             pltpu.VMEM((q, width), f32),
             pltpu.VMEM((depth - 1, e, width), f32),
+            dma((chunks,)),
             dma((chunks,)),
             dma((chunks * (reals - 1),)),
             dma((chunks * (reals - 1),)),
@@ -330,20 +342,28 @@
 
 
 def core_kernel(
-    reals, held_ref, basis_ref, last_ref, got_ref, corner_ref,
-    sending, work, out, send_sem, recv_sem,
+    reals, parts, stored_ref, basis_ref, last_ref, got_ref, corner_ref,
+    held_ref, sending, work, out, load_sem, send_sem, recv_sem,
 ):
     r, cell = lax.axis_index("real"), lax.axis_index("cell")
+    rows, width = stored_ref.shape[1:]
+    count = rows // parts
+    loads = []
+    for part in range(parts):
+        place = pl.ds(part * count, count)
+        load = pltpu.make_async_copy(
+            stored_ref.at[:, place], held_ref.at[:, place], load_sem.at[part]
+        )
+        load.start()
+        loads.append(load)
     peers = [lax.rem(r + d, reals) for d in range(1, reals)]
     places = [{"real": q, "cell": cell} for q in peers]
     greet(places)
-    rows, width = held_ref.shape[1:]
     ranks = got_ref.shape[1]
-    parts = 4
-    count = rows // parts
     copies = []
     for part in range(parts):
         first = part * count
+        loads[part].wait()
         value = mm(held_ref[0, first : first + count, :], basis_ref[:width, :])
         for s in range(1, reals):
             value = value + mm(
@@ -380,24 +400,28 @@
     rank = basis.shape[1]
     size = last.shape[0]
     shape = (reals, rank // reals, rows)
+    parts = 4
+    dma = pltpu.SemaphoreType.DMA
     vmem = pl.BlockSpec(memory_space=pltpu.VMEM)
     return pl.pallas_call(
-        functools.partial(core_kernel, reals),
+        functools.partial(core_kernel, reals, parts),
         out_shape=(
             jax.ShapeDtypeStruct(shape, jnp.float32),
             jax.ShapeDtypeStruct(last.shape, jnp.float32),
         ),
-        in_specs=[vmem] * 3,
+        in_specs=[pl.BlockSpec(memory_space=pl.ANY), vmem, vmem],
         out_specs=[vmem] * 2,
         scratch_shapes=[
+            pltpu.VMEM(held.shape, jnp.float32),
             pltpu.VMEM(shape, jnp.float32),
             pltpu.VMEM((size, 2 * size), jnp.float32),
             pltpu.VMEM((size, 2 * size), jnp.float32),
-            pltpu.SemaphoreType.DMA((4 * (reals - 1),)),
-            pltpu.SemaphoreType.DMA((4 * (reals - 1),)),
+            dma((parts,)),
+            dma((parts * (reals - 1),)),
+            dma((parts * (reals - 1),)),
         ],
         compiler_params=pltpu.CompilerParams(
-            collective_id=1, has_side_effects=True, vmem_limit_bytes=40 * 1024 * 1024
+            collective_id=1, has_side_effects=True, vmem_limit_bytes=60 * 1024 * 1024
         ),
     )(held, basis, last)
 

time: 134 us -> 134 us (level)
    pallas_call x1, Pallas kernels: 16.2 us -> 18.2 us  [projected(): pl.pallas_call(functools.partial(core_kernel, reals, parts), out_shape=(j...]
where the time goes in v5:
time: 134 us
  Pallas kernels  129 us (96%)
  local copies, waits for them, and re-layouts  4.4 us (3%)
    pallas_call x1, Pallas kernels, gathered_gram(): pl.pallas_call(functools.partial(gram_kernel, reals, depth, chunks), out_...  76.4 us
    pallas_call x1, Pallas kernels, factors(): pl.pallas_call(factors_kernel, out_shape=(jax.ShapeDtypeStruct((total, si...  32.8 us
    pallas_call x1, Pallas kernels, projected(): pl.pallas_call(functools.partial(core_kernel, reals, parts), out_shape=(j...  18.2 us
    unnamed x8, local copies, waits for them, and re-layouts  2.93 us

profile of v5, /device:TPU:0, one launch (start us, length us, event | category | flops | bytes accessed | tf_op | source)
XLA Modules:
  0.0 133.7 jit_solution(14701320249081802157)
XLA Ops:
  0.6 0.0 copy-start.2
  0.6 76.4 %shard_map.49 = (f32[4,32,64,128]{3,2,1,0:T(8,128)}, f32[1280,128]{1,0:T(8,128)}) custom-call(f32[32,256,128]{2,1,0:T(8,128)} %field_ref.1), custom_call_target="tpu_custom_call" | custom-call | tf_op jit(solution)/shard_map/pallas_call | solution.py:312
  77.0 0.0 copy-done.2
  77.0 0.0 copy-start.1
  77.0 1.1 copy-done.1
  78.1 32.8 %shard_map.50 = (f32[512,128]{1,0:T(8,128)}, f32[512,512]{1,0:T(8,128)}, f32[128,128]{1,0:T(8,128)S(1)}) custom-call(f32[1280,128]{1,0:T(8,128)S(1)} %copy-done.1, f32[512,128]{1,0:T(8,128)S(1)} %copy-done.2), custom_call_target="tpu_custom_call" | custom-call | tf_op jit(solution)/shard_map/pallas_call | solution.py:146
  110.9 0.0 copy-start.3
  110.9 0.6 copy-done.3
  111.5 18.2 %shard_map.51 = (f32[4,32,2048]{2,1,0:T(8,128)}, f32[128,128]{1,0:T(8,128)}) custom-call(f32[4,2048,128]{2,1,0:T(8,128)} %bitcast.2, f32[512,128]{1,0:T(8,128)} %get-tuple-element.8.basis_ref, f32[128,128]{1,0:T(8,128)} %copy-done.3), custom_call_target="tpu_custom_call" | custom-call | tf_op jit(solution)/shard_map/pallas_call | solution.py:406
  129.7 0.0 copy-start
  129.7 1.2 copy-done
  130.9 1.3 shard_map.52
  132.2 1.5 %constant_dynamic-update-slice_fusion = f32[512,512]{1,0:T(8,128)} fusion(f32[512,512]{1,0:T(8,128)} %get-tuple-element.15, f32[128,128]{1,0:T(8,128)} %get-tuple-element.16), kind=kLoop, calls=%fused_computation | loop fusion | bytes 131072 | tf_op jit(solution)/shard_map/dynamic_update_slice | solution.py:458
Async XLA Ops:
  0.6 76.4 %copy-start.2 = (f32[512,128]{1,0:T(8,128)S(1)}, f32[512,128]{1,0:T(8,128)}, u32[]{:S(2)}) copy-start(f32[512,128]{1,0:T(8,128)} %seed_ref.1) | copy-start | bytes 786436
  77.0 1.1 copy-start.1
  110.9 0.6 copy-start.3
  129.7 1.2 copy-start
